TPU v7x, 128 devices: a whole 4x4x4 slice. The times are simulated.
128 devices in a mesh: dp: 16 (over z, y), code: 8 (over x, core).
Axes of the slice: x: 4, y: 4, z: 4, core: 2. Of those that a mesh axis runs over, the one named last changes fastest.
Arguments:
- vectors: float32 [65536, 256], P('dp'), may hold values from -16 to 16
- codebook: float32 [32768, 256], P('code'), may hold values from -6 to 6
- cand_blocks: int32 [64, 8, 2], P('dp', 'code'), may hold values from 0 to 3, as said below
- cand_counts: int32 [64, 8], P('dp', 'code'), may hold values from 1 to 2
Outputs:
- centroids: float32 [32768, 256], P(('code', 'dp'))
Inputs may be any that keep to these rules, and one draw needn't show every extreme that they name: `cand_blocks`: within one list the first cand_counts entries are distinct.
All inputs are finite; a program needn't handle non-finite values.
Results may differ from a plain program's by a relative error of at most 0.0003.
Values sent between devices are 32-bit elements; how exact they have to be, the bound alone decides.
A program may use at most 128 MiB of HBM per device.

v0:
```python
import jax
import jax.numpy as jnp
from jax import lax
from jax.sharding import PartitionSpec as P

RB = 1024
CB = 1024
ITERS = 3


TEMPER = 4.0
SLACK = 3.0


def local(vectors, codebook, cand_blocks, cand_counts):
    width = vectors.shape[1]
    rblk = vectors.shape[0] // RB
    cblk = codebook.shape[0] // CB
    slots = cand_blocks.shape[2]
    rows = vectors.reshape(rblk, RB, width)
    books = codebook.reshape(cblk, CB, width)
    blocks = cand_blocks[:, 0, :]
    valid = jnp.arange(slots, dtype=jnp.int32)[None, :] < cand_counts
    picked = books[blocks]
    dots = jnp.einsum("rid,rscd->rsic", rows, picked, precision=lax.Precision.HIGHEST)
    cost = (
        jnp.sum(rows * rows, -1)[:, None, :, None]
        + jnp.sum(picked * picked, -1)[:, :, None, :]
        - 2.0 * dots
    ) / TEMPER
    selector = (
        (blocks[:, :, None] == jnp.arange(cblk, dtype=jnp.int32)[None, None, :]) & valid[:, :, None]
    ).astype(jnp.float32)
    chosen = selector[..., None] > 0.0
    potential_v = jnp.zeros((cblk, CB), jnp.float32)
    potential_u = jnp.zeros((rblk, RB), jnp.float32)
    for step in range(ITERS):
        score = jnp.where(
            valid[:, :, None, None], potential_v[blocks][:, :, None, :] - cost, -jnp.inf
        )
        local_top = jnp.max(score, axis=(1, 3))
        row_top = lax.pmax(local_top, "code")
        row_mass = lax.psum(
            jnp.sum(jnp.exp(score - row_top[:, None, :, None]), axis=(1, 3)), "code"
        )
        potential_u = -(row_top + jnp.log(row_mass))
        shifted = potential_u[:, None, :, None] - cost
        tile_top = jnp.where(valid[:, :, None], jnp.max(shifted, axis=2), -jnp.inf)
        block_top = jnp.max(jnp.where(chosen, tile_top[:, :, None, :], -jnp.inf), axis=(0, 1))
        block_top = jnp.maximum(block_top, -SLACK)
        peak = lax.pmax(block_top, "dp")
        expo = jnp.sum(jnp.exp(shifted - peak[blocks][:, :, None, :]), axis=2)
        expo = jnp.where(valid[:, :, None], expo, 0.0)
        mass = lax.psum(
            jnp.einsum("rsb,rsc->bc", selector, expo, precision=lax.Precision.HIGHEST), "dp"
        )
        potential_v = -(peak + jnp.log(mass + jnp.exp(-SLACK - peak)))
    weight = jnp.exp(potential_u[:, None, :, None] + potential_v[blocks][:, :, None, :] - cost)
    weight = jnp.where(valid[:, :, None, None], weight, 0.0)
    partial_sums = jnp.einsum("rsic,rid->rscd", weight, rows, precision=lax.Precision.HIGHEST)
    block_sums = jnp.einsum(
        "rsb,rscd->bcd", selector, partial_sums, precision=lax.Precision.HIGHEST
    )
    total = lax.psum_scatter(
        block_sums.reshape(cblk * CB, width), "dp", scatter_dimension=0, tiled=True
    )
    own_rows = total.shape[0]
    begin = lax.axis_index("dp") * own_rows
    own_books = lax.dynamic_slice_in_dim(codebook, begin, own_rows, 0)
    own_v = lax.dynamic_slice_in_dim(potential_v.reshape(-1), begin, own_rows, 0)
    return total + jnp.exp(own_v - SLACK)[:, None] * own_books


def solution(mesh):
    return jax.shard_map(
        local,
        mesh=mesh,
        in_specs=(P("dp", None), P("code", None), P("dp", "code", None), P("dp", "code")),
        out_specs=P(("code", "dp"), None),
        check_vma=False,
    )
```

profile of v0, /device:TPU:0, one launch (start us, length us, event | category | flops | bytes accessed | tf_op | source)
XLA Modules:
  0.0 913.2 jit_solution(2510734819995223698)
XLA Ops:
  8.1 6.5 gather_fusion.1
  14.6 4.6 multiply_reduce_fusion
  19.8 2.8 multiply_reduce_fusion.1
  22.7 38.8 %fusion.6 = (f32[4,1024]{1,0:T(4,128)S(1)}, f32[4,2,1024,1024]{2,3,1,0:T(8,128)}) fusion(f32[4,2,1024]{2,1,0:T(2,128)S(1)} %reshape.124, pred[4,2]{1,0:T(4,128)(4,1)S(1)} %iota_compare_fusion.1, f32[4,2,1024,256]{3,2,1,0:T(8,128)} %bitcast.41, f32[4,1024,256,1]{2,1,3,0:T(8,128)} %bitcast.45, f32[4,2,1024]{2,1,0:T(2,128)S(1)} %multiply_reduce_fusion, ...), kind=kOutput, calls=%fused_computation.27 | convolution fusion | flops 25828519936 | bytes 46235656 | tf_op jit(solution)/shard_map/rid,rscd->rsic/dot_general | solution.py:25
  61.5 26.0 %pmax.42 = f32[4,1024]{1,0:T(4,128)S(1)} all-reduce(f32[4,1024]{1,0:T(4,128)S(1)} %get-tuple-element.7), channel_id=1, replica_groups=mesh['dp'=16,'code'=8] {'code'}, use_global_device_ids=true, to_apply=%region_3.4 | all-reduce | flops 4096 | bytes 32768 | tf_op jit(solution)/shard_map/pmax | solution.py:42
  87.5 14.3 %exponential_reduce_fusion.5 = f32[4,1024]{1,0:T(4,128)S(1)} fusion(f32[4,2,1024,1024]{2,3,1,0:T(8,128)} %get-tuple-element.8, f32[4,1024]{1,0:T(4,128)S(1)} %pmax.42, f32[4,2,1024]{2,1,0:T(2,128)S(1)} %reshape.124, pred[4,2]{1,0:T(4,128)(4,1)S(1)} %iota_compare_fusion.1), kind=kLoop, calls=%fused_computation.22 | loop fusion | flops 33550336 | bytes 33619976 | tf_op jit(solution)/shard_map/reduce_sum | solution.py:44
  101.8 23.6 %psum.42 = f32[4,1024]{1,0:T(4,128)S(1)} all-reduce(f32[4,1024]{1,0:T(4,128)S(1)} %exponential_reduce_fusion.5), channel_id=1, replica_groups=mesh['dp'=16,'code'=8] {'code'}, use_global_device_ids=true, to_apply=%region_5.6 | all-reduce | flops 4096 | bytes 32768 | tf_op jit(solution)/shard_map/psum | solution.py:43
  125.4 12.2 %subtract_reduce_fusion.2 = f32[4,2,1024]{2,1,0:T(2,128)S(1)} fusion(f32[4,2,1024,1024]{2,3,1,0:T(8,128)} %get-tuple-element.8, f32[4,1024]{1,0:T(4,128)S(1)} %add_negate_fusion.5), kind=kLoop, calls=%fused_computation.26 | loop fusion | flops 16769024 | bytes 33603584 | tf_op jit(solution)/shard_map/reduce_max | solution.py:48
  138.0 75.9 %pmax.43 = f32[4,1024]{1,0:T(4,128)S(1)} all-reduce(f32[4,1024]{1,0:T(4,128)S(1)} %broadcast_maximum_fusion.2), channel_id=1, replica_groups=mesh['dp'=16,'code'=8] {'dp'}, use_global_device_ids=true, to_apply=%region_8.9 | all-reduce | flops 4096 | bytes 32768 | tf_op jit(solution)/shard_map/pmax | solution.py:51
  214.5 14.2 %exponential_reduce_fusion.4 = f32[4,2,1024]{2,1,0:T(2,128)S(1)} fusion(f32[4,2,1024,1024]{2,3,1,0:T(8,128)} %get-tuple-element.8, f32[4,2,1024]{2,1,0:T(2,128)S(1)} %reshape.140, f32[4,1024]{1,0:T(4,128)S(1)} %add_negate_fusion.5), kind=kLoop, calls=%fused_computation.21 | loop fusion | flops 25157632 | bytes 33636352 | tf_op jit(solution)/shard_map/reduce_sum | solution.py:52
  229.0 69.5 %psum.43 = f32[4,1024]{1,0:T(4,128)S(1)} all-reduce(f32[4,1024]{1,0:T(4,128)S(1)} %convolution_bitcast_fusion.2), channel_id=1, replica_groups=mesh['dp'=16,'code'=8] {'dp'}, use_global_device_ids=true, to_apply=%region_10.11 | all-reduce | flops 4096 | bytes 32768 | tf_op jit(solution)/shard_map/psum | solution.py:54
  299.2 12.8 %fusion.7 = f32[4,1024]{1,0:T(4,128)S(1)} fusion(f32[4,2,1024,1024]{2,3,1,0:T(8,128)} %get-tuple-element.8, f32[4,2,1024]{2,1,0:T(2,128)S(1)} %reshape.148, pred[4,2]{1,0:T(4,128)(4,1)S(1)} %iota_compare_fusion.1), kind=kLoop, calls=%fused_computation.28 | loop fusion | flops 25161728 | bytes 33603592 | tf_op jit(solution)/shard_map/reduce_max | solution.py:41
  311.9 23.6 %pmax.44 = f32[4,1024]{1,0:T(4,128)S(1)} all-reduce(f32[4,1024]{1,0:T(4,128)S(1)} %fusion.7), channel_id=1, replica_groups=mesh['dp'=16,'code'=8] {'code'}, use_global_device_ids=true, to_apply=%region_12.13 | all-reduce | flops 4096 | bytes 32768 | tf_op jit(solution)/shard_map/pmax | solution.py:42
  335.5 14.3 %exponential_reduce_fusion.3 = f32[4,1024]{1,0:T(4,128)S(1)} fusion(f32[4,2,1024,1024]{2,3,1,0:T(8,128)} %get-tuple-element.8, f32[4,1024]{1,0:T(4,128)S(1)} %pmax.44, f32[4,2,1024]{2,1,0:T(2,128)S(1)} %reshape.148, pred[4,2]{1,0:T(4,128)(4,1)S(1)} %iota_compare_fusion.1), kind=kLoop, calls=%fused_computation.19 | loop fusion | flops 33550336 | bytes 33619976 | tf_op jit(solution)/shard_map/reduce_sum | solution.py:44
  349.8 23.6 %psum.44 = f32[4,1024]{1,0:T(4,128)S(1)} all-reduce(f32[4,1024]{1,0:T(4,128)S(1)} %exponential_reduce_fusion.3), channel_id=1, replica_groups=mesh['dp'=16,'code'=8] {'code'}, use_global_device_ids=true, to_apply=%region_14.15 | all-reduce | flops 4096 | bytes 32768 | tf_op jit(solution)/shard_map/psum | solution.py:43
  373.4 12.2 %subtract_reduce_fusion.1 = f32[4,2,1024]{2,1,0:T(2,128)S(1)} fusion(f32[4,2,1024,1024]{2,3,1,0:T(8,128)} %get-tuple-element.8, f32[4,1024]{1,0:T(4,128)S(1)} %add_negate_fusion.3), kind=kLoop, calls=%fused_computation.25 | loop fusion | flops 16769024 | bytes 33603584 | tf_op jit(solution)/shard_map/reduce_max | solution.py:48
  385.8 69.5 %pmax.45 = f32[4,1024]{1,0:T(4,128)S(1)} all-reduce(f32[4,1024]{1,0:T(4,128)S(1)} %broadcast_maximum_fusion.1), channel_id=1, replica_groups=mesh['dp'=16,'code'=8] {'dp'}, use_global_device_ids=true, to_apply=%region_17.18 | all-reduce | flops 4096 | bytes 32768 | tf_op jit(solution)/shard_map/pmax | solution.py:51
  455.9 14.2 %exponential_reduce_fusion.2 = f32[4,2,1024]{2,1,0:T(2,128)S(1)} fusion(f32[4,2,1024,1024]{2,3,1,0:T(8,128)} %get-tuple-element.8, f32[4,2,1024]{2,1,0:T(2,128)S(1)} %reshape.156, f32[4,1024]{1,0:T(4,128)S(1)} %add_negate_fusion.3), kind=kLoop, calls=%fused_computation.18 | loop fusion | flops 25157632 | bytes 33636352 | tf_op jit(solution)/shard_map/reduce_sum | solution.py:52
  470.5 69.5 %psum.45 = f32[4,1024]{1,0:T(4,128)S(1)} all-reduce(f32[4,1024]{1,0:T(4,128)S(1)} %convolution_bitcast_fusion.1), channel_id=1, replica_groups=mesh['dp'=16,'code'=8] {'dp'}, use_global_device_ids=true, to_apply=%region_19.20 | all-reduce | flops 4096 | bytes 32768 | tf_op jit(solution)/shard_map/psum | solution.py:54
  540.6 12.8 %fusion.8 = f32[4,1024]{1,0:T(4,128)S(1)} fusion(f32[4,2,1024,1024]{2,3,1,0:T(8,128)} %get-tuple-element.8, f32[4,2,1024]{2,1,0:T(2,128)S(1)} %reshape.164, pred[4,2]{1,0:T(4,128)(4,1)S(1)} %iota_compare_fusion.1), kind=kLoop, calls=%fused_computation.29 | loop fusion | flops 25161728 | bytes 33603592 | tf_op jit(solution)/shard_map/reduce_max | solution.py:41
  553.4 23.6 %pmax.46 = f32[4,1024]{1,0:T(4,128)S(1)} all-reduce(f32[4,1024]{1,0:T(4,128)S(1)} %fusion.8), channel_id=1, replica_groups=mesh['dp'=16,'code'=8] {'code'}, use_global_device_ids=true, to_apply=%region_21.22 | all-reduce | flops 4096 | bytes 32768 | tf_op jit(solution)/shard_map/pmax | solution.py:42
  577.0 14.3 %exponential_reduce_fusion.1 = f32[4,1024]{1,0:T(4,128)S(1)} fusion(f32[4,2,1024,1024]{2,3,1,0:T(8,128)} %get-tuple-element.8, f32[4,1024]{1,0:T(4,128)S(1)} %pmax.46, f32[4,2,1024]{2,1,0:T(2,128)S(1)} %reshape.164, pred[4,2]{1,0:T(4,128)(4,1)S(1)} %iota_compare_fusion.1), kind=kLoop, calls=%fused_computation.16 | loop fusion | flops 33550336 | bytes 33619976 | tf_op jit(solution)/shard_map/reduce_sum | solution.py:44
  591.3 23.6 %psum.46 = f32[4,1024]{1,0:T(4,128)S(1)} all-reduce(f32[4,1024]{1,0:T(4,128)S(1)} %exponential_reduce_fusion.1), channel_id=1, replica_groups=mesh['dp'=16,'code'=8] {'code'}, use_global_device_ids=true, to_apply=%region_23.24 | all-reduce | flops 4096 | bytes 32768 | tf_op jit(solution)/shard_map/psum | solution.py:43
  614.9 12.2 %subtract_reduce_fusion = f32[4,2,1024]{2,1,0:T(2,128)S(1)} fusion(f32[4,2,1024,1024]{2,3,1,0:T(8,128)} %get-tuple-element.8, f32[4,1024]{1,0:T(4,128)S(1)} %add_negate_fusion.1), kind=kLoop, calls=%fused_computation.24 | loop fusion | flops 16769024 | bytes 33603584 | tf_op jit(solution)/shard_map/reduce_max | solution.py:48
  627.3 69.5 %pmax.47 = f32[4,1024]{1,0:T(4,128)S(1)} all-reduce(f32[4,1024]{1,0:T(4,128)S(1)} %broadcast_maximum_fusion), channel_id=1, replica_groups=mesh['dp'=16,'code'=8] {'dp'}, use_global_device_ids=true, to_apply=%region_26.27 | all-reduce | flops 4096 | bytes 32768 | tf_op jit(solution)/shard_map/pmax | solution.py:51
  697.4 14.2 %exponential_reduce_fusion = f32[4,2,1024]{2,1,0:T(2,128)S(1)} fusion(f32[4,2,1024,1024]{2,3,1,0:T(8,128)} %get-tuple-element.8, f32[4,2,1024]{2,1,0:T(2,128)S(1)} %reshape.172, f32[4,1024]{1,0:T(4,128)S(1)} %add_negate_fusion.1), kind=kLoop, calls=%fused_computation.15 | loop fusion | flops 25157632 | bytes 33636352 | tf_op jit(solution)/shard_map/reduce_sum | solution.py:52
  712.0 69.7 %psum.47 = f32[4,1024]{1,0:T(4,128)S(1)} all-reduce(f32[4,1024]{1,0:T(4,128)S(1)} %convolution_bitcast_fusion), channel_id=1, replica_groups=mesh['dp'=16,'code'=8] {'dp'}, use_global_device_ids=true, to_apply=%region_28.29 | all-reduce | flops 4096 | bytes 32768 | tf_op jit(solution)/shard_map/psum | solution.py:54
  782.3 36.8 %fusion.1 = f32[4,2,1024,256]{3,2,1,0:T(8,128)S(1)} fusion(f32[4,1024,256,1]{2,1,3,0:T(8,128)} %bitcast.46, f32[4,2,1024,1024]{2,3,1,0:T(8,128)} %get-tuple-element.8, f32[4,2,1024]{2,1,0:T(2,128)S(1)} %reshape.180, f32[4,1024]{1,0:T(4,128)S(1)} %add_negate_fusion.1, pred[4,2]{1,0:T(4,128)(4,1)S(1)} %iota_compare_fusion.1), kind=kOutput, calls=%fused_computation.10 | convolution fusion | flops 25794969600 | bytes 46186504 | tf_op jit(solution)/shard_map/rsic,rid->rscd/dot_general | solution.py:60
  819.2 10.9 %fusion.15 = f32[4,1024,256]{2,0,1:T(4,128)S(1)} fusion(f32[4,2,1024,256]{3,2,1,0:T(8,128)S(1)} %fusion.1, pred[4,2,4]{0,2,1:T(4,128)(4,1)S(1)} %get-tuple-element.6), kind=kOutput, calls=%fused_computation.38 | convolution fusion | flops 100663296 | bytes 12582944 | tf_op jit(solution)/shard_map/rsb,rscd->bcd/dot_general | solution.py:61
  830.1 2.7 copy.35
  832.9 71.2 %reduce-scatter.2.cloned.1.call-done = f32[256,256]{1,0:T(8,128)} async-done(((f32[4096,256]{1,0:T(8,128)}), f32[256,256]{1,0:T(8,128)}) %reduce-scatter.2.cloned.1.call-update) | async-done | bytes 262160 | tf_op jit(solution)/shard_map/reduce_scatter | solution.py:64
  904.1 1.8 multiply_add_fusion
  (51 shorter events, 7.7 us)
Async XLA Ops:
  6.5 897.5 %reduce-scatter.2.cloned.1.call-start = ((), (), s32[]{:S(2)}) async-start(), calls=%async_computation.1 | async-start | bytes 4456448 | tf_op jit(solution)/shard_map/reduce_scatter | solution.py:64
  87.5 50.2 %copy-start = (s32[4,1,2]{0,2,1:T(2,128)S(1)}, s32[4,1,2]{0,2,1:T(2,128)}, u32[]{:S(2)}) copy-start(s32[4,1,2]{0,2,1:T(2,128)} %param.6) | copy-start | bytes 100
Sparse Core Ops, SparseCore 0:
  832.9 71.1 reduce-scatter.1
where the time goes:
time: 923 us; the launch traced here: 913 us
  blocking collectives  567 us (61%)
  other arithmetic  159 us (17%)
  matrix products  87.2 us (9%)
  waiting for transfers between devices  71.2 us (8%)
  between operations  14.1 us (2%)
  local copies, waits for them, and re-layouts  13.7 us (1%)
    pmax x3, blocking collectives, local(): peak = lax.pmax(block_top, 'dp')  215 us
    psum x3, blocking collectives, local(): lax.psum(jnp.einsum('rsb,rsc->bc', selector, expo, precision=lax.Precisio...  209 us
    pmax x3, blocking collectives, local(): row_top = lax.pmax(local_top, 'code')  73.1 us
    reduce_scatter x1, waiting for transfers between devices, local(): lax.psum_scatter(block_sums.reshape(cblk * CB, width), 'dp', scatter_dime...  71.2 us
    psum x3, blocking collectives, local(): lax.psum(jnp.sum(jnp.exp(score - row_top[:, None, :, None]), axis=(1, 3))...  70.7 us
    reduce_sum x3, other arithmetic, local(): jnp.sum(jnp.exp(score - row_top[:, None, :, None]), axis=(1, 3))  42.9 us
    reduce_sum x3, other arithmetic, local(): expo = jnp.sum(jnp.exp(shifted - peak[blocks][:, :, None, :]), axis=2)  42.7 us
    dot_general x1, matrix products, local(): jnp.einsum('rid,rscd->rsic', rows, picked, precision=lax.Precision.HIGHEST)  38.8 us
  transfers between devices with their start and end apart: 1, of which 1 were waited for; matrix products, arithmetic and copies ran while one was open for 0% of the time, Pallas kernels for 0%

commit v1 on v0

v1 whole, which is shorter than its diff:
```python
import functools
import math

import jax
import jax.numpy as jnp
from jax import lax
from jax.experimental import pallas as pl
from jax.experimental.pallas import tpu as pltpu
from jax.sharding import PartitionSpec as P

MESH = pl.DeviceIdType.MESH
LOG2E = 1.0 / math.log(2.0)
EPS = math.exp(-3.0)
F32 = jnp.float32
BF16 = jnp.bfloat16
NT = (((1,), (1,)), ((), ()))


def split(v):
    hi = v.astype(BF16)
    return hi, (v - hi.astype(F32)).astype(BF16)


def repeat8(a):
    return jnp.concatenate([a] * 8, axis=1)


def wait_bytes(ref, sem):
    pltpu.make_async_copy(ref, ref, sem).wait()


def kernel(
    blocks, counts, x_ref, c_hbm, out_ref,
    e, s, ccat, bias, arep, prod, cown,
    rg0, rg, alpha, gvec, cols, zg, yg, msum, y1, z1, u0, u1,
    c_sem, r_send, r_recv, d_send, d_recv, p_send, p_recv,
):
    dp = lax.axis_index("dp")
    code = lax.axis_index("code")
    z, y = dp // 4, dp % 4

    def code_peer(d):
        return (dp, (code + d) % 8)

    def z_peer(d):
        return (((z + d) % 4) * 4 + y, code)

    def y_peer(d):
        return (z * 4 + (y + d) % 4, code)

    def push(src, dst, send, recv, peer):
        pltpu.make_async_remote_copy(
            src_ref=src, dst_ref=dst, send_sem=send, recv_sem=recv,
            device_id=peer, device_id_type=MESH,
        ).start()

    for h in range(2):
        for p in range(4):
            for q in range(4):
                pltpu.make_async_copy(
                    c_hbm.at[:, q, p, :, pl.ds(h * 128, 128)],
                    s.at[h, :, p, pl.ds(q * 64, 64), :],
                    c_sem.at[0],
                ).start()
    own_copy = pltpu.make_async_copy(c_hbm.at[z, y], cown, c_sem.at[1])
    own_copy.start()

    barrier = pltpu.get_barrier_semaphore()
    for d in range(1, 8):
        pl.semaphore_signal(barrier, inc=1, device_id=code_peer(d), device_id_type=MESH)
    for d in range(1, 4):
        pl.semaphore_signal(barrier, inc=1, device_id=z_peer(d), device_id_type=MESH)
        pl.semaphore_signal(barrier, inc=1, device_id=y_peer(d), device_id_type=MESH)

    wait_bytes(s, c_sem.at[0])

    def prepare(n, carry):
        b, p = n // 4, n % 4
        c0 = s[0, b, p]
        c1 = s[1, b, p]
        norm = jnp.sum(c0 * c0 + c1 * c1, axis=1, keepdims=True) * (-0.25 * LOG2E)
        rows = pl.ds(pl.multiple_of(p * 256, 256), 256)
        bias[b, rows, :] = jnp.broadcast_to(norm, (256, 128))
        for h, part in enumerate((c0, c1)):
            hi, lo = split(part * (0.5 * LOG2E))
            ccat[b, rows, h * 128:(h + 1) * 128] = hi
            ccat[b, rows, 256 + h * 128:256 + (h + 1) * 128] = lo
        return carry

    lax.fori_loop(0, 16, prepare, 0)

    def stage(n, carry):
        r, iq = n // 4, n % 4
        rows = pl.ds(pl.multiple_of(n * 256, 256), 256)
        cols_i = pl.ds(pl.multiple_of(iq * 256, 256), 256)
        xh, xl = split(x_ref[rows, :])
        xcat = jnp.concatenate([xh, xl, xh], axis=1)
        top = None
        for slot in range(2):
            b = blocks[r, slot]
            ch = ccat[b, :, 0:256]
            cl = ccat[b, :, 256:512]
            lhs = jnp.concatenate([ch, ch, cl], axis=1)
            score = lax.dot_general(lhs, xcat, NT, preferred_element_type=F32)
            bb = bias[b]
            score = score + jnp.concatenate([bb, bb], axis=1)
            e[r * 2 + slot, :, cols_i] = score
            peak = jnp.max(score, axis=0, keepdims=True)
            if slot == 0:
                top = peak
            else:
                top = jnp.where(counts[r] > 1, jnp.maximum(top, peak), top)
        total = jnp.zeros((8, 256), F32)
        for slot in range(2):
            shift = top if slot == 0 else jnp.where(counts[r] > 1, top, 3e38)
            w = jnp.exp2(e[r * 2 + slot, :, cols_i] - shift)
            e[r * 2 + slot, :, cols_i] = w
            total = total + jnp.sum(w.reshape(128, 8, 256), axis=0)
        rg0[r, code, :, cols_i] = top
        rg0[r, code, :, pl.ds(pl.multiple_of(1024 + iq * 256, 256), 256)] = jnp.sum(
            total, axis=0, keepdims=True
        )
        return carry

    def row_first(r, carry):
        lax.fori_loop(r * 4, r * 4 + 4, stage, 0)

        @pl.when(r == 0)
        def _():
            pl.semaphore_wait(barrier, 13)

        for d in range(1, 8):
            push(rg0.at[r, code], rg0.at[r, code], r_send.at[0, r], r_recv.at[0, r], code_peer(d))
        return carry

    lax.fori_loop(0, 4, row_first, 0)

    def col_block(r):
        g = repeat_rows(gvec[r])
        for slot in range(2):
            def chunk(n, carry):
                k = pl.ds(pl.multiple_of(n * 128, 128), 128)
                w = e[r * 2 + slot, k, :] * g
                acc = w[:, 0:128]
                for j in range(1, 8):
                    acc = acc + w[:, j * 128:(j + 1) * 128]
                cols[r * 2 + slot, :, k] = jnp.sum(acc.T, axis=0, keepdims=True)
                return carry

            lax.fori_loop(0, 8, chunk, 0)

    def repeat_rows(v):
        return jnp.broadcast_to(v, (128, 1024))

    def col_first(r, carry):
        wait_bytes(rg0.at[r, pl.ds(0, 7)], r_recv.at[0, r])
        tops = [rg0[r, j, :, 0:1024] for j in range(8)]
        best = functools.reduce(jnp.maximum, tops)
        total = jnp.zeros((1, 1024), F32)
        for j in range(8):
            total = total + jnp.exp2(tops[j] - best) * rg0[r, j, :, 1024:2048]
        mine = jnp.exp2(rg0[r, code, :, 0:1024] - best)
        alpha[r] = mine
        gvec[r] = mine / total
        col_block(r)
        return carry

    def col_next(it):
        def body(r, carry):
            wait_bytes(rg.at[it, r, pl.ds(0, 7)], r_recv.at[it + 1, r])
            total = rg[it, r, 0]
            for j in range(1, 8):
                total = total + rg[it, r, j]
            gvec[r] = alpha[r] / total
            col_block(r)
            return carry

        return body

    def row_next(it):
        def body(r, carry):
            acc = jnp.zeros((8, 1024), F32)
            for slot in range(2):
                b = blocks[r, slot]

                def chunk(n, acc):
                    k = pl.ds(pl.multiple_of(n * 64, 64), 64)
                    w = e[r * 2 + slot, k, :] * repeat8(arep[b, k, :])
                    return acc + jnp.sum(w.reshape(8, 8, 1024), axis=0)

                acc = lax.fori_loop(0, 16, chunk, acc)
            rg[it, r, code] = jnp.sum(acc, axis=0, keepdims=True) * alpha[r]
            for d in range(1, 8):
                push(
                    rg.at[it, r, code], rg.at[it, r, code],
                    r_send.at[it + 1, r], r_recv.at[it + 1, r], code_peer(d),
                )
            return carry

        return body

    def has_slot(r, b):
        second = (blocks[r, 1] == b) & (counts[r] > 1)
        slot = jnp.where(second, 1, 0)
        has = second | (blocks[r, 0] == b)
        return has, slot

    def dp_sum(it):
        for b in range(4):
            total = jnp.zeros((1, 1024), F32)
            for r in range(4):
                has, slot = has_slot(r, b)
                total = total + jnp.where(has, cols[r * 2 + slot], 0.0)
            zg[it, z, b] = total
        for d in range(1, 4):
            push(zg.at[it, z], zg.at[it, z], d_send.at[0, it], d_recv.at[0, it], z_peer(d))

    def dp_mid(it):
        wait_bytes(zg.at[it, pl.ds(0, 3)], d_recv.at[0, it])
        for b in range(4):
            yg[it, y, b] = (zg[it, 0, b] + zg[it, 1, b]) + (zg[it, 2, b] + zg[it, 3, b])
        for d in range(1, 4):
            push(yg.at[it, y], yg.at[it, y], d_send.at[1, it], d_recv.at[1, it], y_peer(d))

    def dp_end(it):
        wait_bytes(yg.at[it, pl.ds(0, 3)], d_recv.at[1, it])
        for b in range(4):
            msum[b] = (yg[it, 0, b] + yg[it, 1, b]) + (yg[it, 2, b] + yg[it, 3, b])

    def spread(v):
        return jnp.broadcast_to(v, (128, 128)).T

    def next_a(it):
        dp_sum(it)
        dp_mid(it)
        dp_end(it)
        for b in range(4):
            msum[b] = 1.0 / (msum[b] + EPS)

        def lay(n, carry):
            b, j = n // 8, n % 8
            k = pl.ds(pl.multiple_of(j * 128, 128), 128)
            arep[b, k, :] = spread(msum[b, :, k])
            return carry

        lax.fori_loop(0, 32, lay, 0)

    lax.fori_loop(0, 4, col_first, 0)
    next_a(0)
    lax.fori_loop(0, 4, row_next(0), 0)
    lax.fori_loop(0, 4, col_next(0), 0)
    next_a(1)
    lax.fori_loop(0, 4, row_next(1), 0)
    lax.fori_loop(0, 4, col_next(1), 0)
    dp_sum(2)

    def scale(n, carry):
        r, j = n // 8, n % 8
        i = pl.ds(pl.multiple_of(j * 128, 128), 128)
        gr = spread(gvec[r, :, i])
        xs = x_ref[pl.ds(pl.multiple_of(n * 128, 128), 128), :] * jnp.concatenate([gr, gr], axis=1)
        hi, lo = split(xs)
        ccat[r, i, 0:256] = hi
        ccat[r, i, 256:512] = lo
        return carry

    lax.fori_loop(0, 32, scale, 0)
    dp_mid(2)

    def reduce_first(p):
        wait_bytes(y1.at[:, p], p_recv.at[0, p])
        wait_bytes(z1.at[:, p], p_recv.at[1, p])
        own = pl.ds(pl.multiple_of(y * 64, 64), 64)
        for b in range(4):
            s[0, b, p, own, :] = (s[0, b, p, own, :] + y1[0, p, b]) + (y1[1, p, b] + y1[2, p, b])
        s[1, z, p] = (s[1, z, p] + z1[0, p]) + (z1[1, p] + z1[2, p])
        for d in range(1, 4):
            push(s.at[0, (z + d) % 4, p, own, :], u0.at[d - 1, p], p_send.at[2, p], p_recv.at[2, p], z_peer(d))
            dest = pl.ds(pl.multiple_of(((y + d) % 4) * 64, 64), 64)
            push(s.at[1, z, p, dest, :], u1.at[d - 1, p], p_send.at[3, p], p_recv.at[3, p], y_peer(d))

    def part(p, carry):
        rows = pl.ds(pl.multiple_of(p * 256, 256), 256)

        def one(r, carry):
            xh = ccat[r, :, 0:256]
            xl = ccat[r, :, 256:512]
            rhs = jnp.concatenate([xh, xl, xh], axis=0)
            for slot in range(2):
                eh, el = split(e[r * 2 + slot, rows, :])
                lhs = jnp.concatenate([eh, eh, el], axis=1)
                prod[r * 2 + slot] = jnp.dot(lhs, rhs, preferred_element_type=F32)
            return carry

        lax.fori_loop(0, 4, one, 0)
        for b in range(4):
            total = jnp.zeros((256, 256), F32)
            for r in range(4):
                has, slot = has_slot(r, b)
                total = total + jnp.where(has, prod[r * 2 + slot], 0.0)
            s[0, b, p] = total[:, 0:128]
            s[1, b, p] = total[:, 128:256]
        for d in range(1, 4):
            dest = pl.ds(pl.multiple_of(((y + d) % 4) * 64, 64), 64)
            push(s.at[0, :, p, dest, :], y1.at[d - 1, p], p_send.at[0, p], p_recv.at[0, p], y_peer(d))
            push(s.at[1, (z + d) % 4, p], z1.at[d - 1, p], p_send.at[1, p], p_recv.at[1, p], z_peer(d))

        @pl.when(p > 0)
        def _():
            reduce_first(p - 1)

        return carry

    lax.fori_loop(0, 4, part, 0)
    dp_end(2)
    own_copy.wait()

    def lay_own(j, carry):
        k = pl.ds(pl.multiple_of(j * 128, 128), 128)
        arep[0, k, :] = spread(1.0 / (msum[z, :, k] + EPS))
        return carry

    lax.fori_loop(0, 8, lay_own, 0)
    reduce_first(3)

    def finish(p, carry):
        wait_bytes(u0.at[:, p], p_recv.at[2, p])
        wait_bytes(u1.at[:, p], p_recv.at[3, p])
        own = pl.ds(pl.multiple_of(y * 64, 64), 64)
        f0 = (s[0, z, p, own, :] + u0[0, p]) + (u0[1, p] + u0[2, p])
        f1 = (s[1, z, p, own, :] + u1[0, p]) + (u1[1, p] + u1[2, p])
        a = arep[0, pl.ds(pl.multiple_of(p * 256 + y * 64, 64), 64), :]
        out_ref[p, :, 0:128] = (f0 + EPS * cown[p, :, 0:128]) * a
        out_ref[p, :, 128:256] = (f1 + EPS * cown[p, :, 128:256]) * a
        return carry

    lax.fori_loop(0, 4, finish, 0)

    def drain_rows(r, carry):
        wait_bytes(rg0.at[r, pl.ds(0, 7)], r_send.at[0, r])
        wait_bytes(rg.at[0, r, pl.ds(0, 7)], r_send.at[1, r])
        wait_bytes(rg.at[1, r, pl.ds(0, 7)], r_send.at[2, r])
        wait_bytes(y1.at[:, r], p_send.at[0, r])
        wait_bytes(z1.at[:, r], p_send.at[1, r])
        wait_bytes(u0.at[:, r], p_send.at[2, r])
        wait_bytes(u1.at[:, r], p_send.at[3, r])
        return carry

    lax.fori_loop(0, 4, drain_rows, 0)
    for it in range(3):
        wait_bytes(zg.at[it, pl.ds(0, 3)], d_send.at[0, it])
        wait_bytes(yg.at[it, pl.ds(0, 3)], d_send.at[1, it])


def local(vectors, codebook, cand_blocks, cand_counts):
    smem = pl.BlockSpec(memory_space=pltpu.SMEM)
    vmem = pl.BlockSpec(memory_space=pltpu.VMEM)
    out = pl.pallas_call(
        kernel,
        out_shape=jax.ShapeDtypeStruct((4, 64, 256), F32),
        in_specs=[smem, smem, vmem, pl.BlockSpec(memory_space=pl.ANY)],
        out_specs=vmem,
        scratch_shapes=[
            pltpu.VMEM((8, 1024, 1024), F32),
            pltpu.VMEM((2, 4, 4, 256, 128), F32),
            pltpu.VMEM((4, 1024, 512), BF16),
            pltpu.VMEM((4, 1024, 128), F32),
            pltpu.VMEM((4, 1024, 128), F32),
            pltpu.VMEM((8, 256, 256), F32),
            pltpu.VMEM((4, 64, 256), F32),
            pltpu.VMEM((4, 8, 1, 2048), F32),
            pltpu.VMEM((2, 4, 8, 1, 1024), F32),
            pltpu.VMEM((4, 1, 1024), F32),
            pltpu.VMEM((4, 1, 1024), F32),
            pltpu.VMEM((8, 1, 1024), F32),
            pltpu.VMEM((3, 4, 4, 1, 1024), F32),
            pltpu.VMEM((3, 4, 4, 1, 1024), F32),
            pltpu.VMEM((4, 1, 1024), F32),
            pltpu.VMEM((3, 4, 4, 64, 128), F32),
            pltpu.VMEM((3, 4, 256, 128), F32),
            pltpu.VMEM((3, 4, 64, 128), F32),
            pltpu.VMEM((3, 4, 64, 128), F32),
            pltpu.SemaphoreType.DMA((2,)),
            pltpu.SemaphoreType.DMA((3, 4)),
            pltpu.SemaphoreType.DMA((3, 4)),
            pltpu.SemaphoreType.DMA((2, 3)),
            pltpu.SemaphoreType.DMA((2, 3)),
            pltpu.SemaphoreType.DMA((4, 4)),
            pltpu.SemaphoreType.DMA((4, 4)),
        ],
        compiler_params=pltpu.CompilerParams(
            collective_id=0, has_side_effects=True, vmem_limit_bytes=63 * 1024 * 1024,
        ),
    )(
        cand_blocks.reshape(4, 2),
        cand_counts.reshape(4),
        vectors,
        codebook.reshape(4, 4, 4, 64, 256),
    )
    return out.reshape(256, 256)


def solution(mesh):
    return jax.shard_map(
        local,
        mesh=mesh,
        in_specs=(P("dp", None), P("code", None), P("dp", "code", None), P("dp", "code")),
        out_specs=P(("code", "dp"), None),
        check_vma=False,
    )
```

time: 923 us -> 132 us (0.14); the launches traced: 913 us -> 132 us
  blocking collectives: 567 us -> 0 us
  other arithmetic: 159 us -> 0 us
  Pallas kernels: 0 us -> 129 us
  matrix products: 87.2 us -> 0 us
  waiting for transfers between devices: 71.2 us -> 0 us
  between operations: 14.1 us -> 0.01 us
  local copies, waits for them, and re-layouts: 13.7 us -> 3.01 us
    pmax x6 -> x0, blocking collectives: 288 us -> none  [the longest x3 215 us: local(): peak = lax.pmax(block_top, 'dp')]
    psum x6 -> x0, blocking collectives: 279 us -> none  [the longest x3 209 us: local(): lax.psum(jnp.einsum('rsb,rsc->bc', selector, expo, precision=lax.Precisio...]
    pallas_call x0 -> x1, Pallas kernels: none -> 129 us  [local(): pl.pallas_call(kernel, out_shape=jax.ShapeDtypeStruct((4, 64, 256), F32),...]
    reduce_sum x8 -> x0, other arithmetic: 93 us -> none  [the longest x3 42.9 us: local(): jnp.sum(jnp.exp(score - row_top[:, None, :, None]), axis=(1, 3))]
    dot_general x6 -> x0, matrix products: 87.2 us -> none  [the longest x1 38.8 us: local(): jnp.einsum('rid,rscd->rsic', rows, picked, precision=lax.Precision.HIGHEST)]
    reduce_scatter x1 -> x0, waiting for transfers between devices: 71.2 us -> none  [local(): lax.psum_scatter(block_sums.reshape(cblk * CB, width), 'dp', scatter_dime...]
    reduce_max x8 -> x0, other arithmetic: 62.5 us -> none  [the longest x3 36.7 us: local(): tile_top = jnp.where(valid[:, :, None], jnp.max(shifted, axis=2), -jnp.inf)]
    gather x15 -> x0, local copies, waits for them, and re-layouts: 10.6 us -> none  [the longest x1 6.47 us: local(): picked = books[blocks]]
  transfers between devices with their start and end apart: 1 -> 0, of which waited for: 1 -> 0; matrix products, arithmetic and copies ran while one was open for 0% -> 0% of each run, Pallas kernels for 0% -> 0%
where the time goes in v1:
time: 132 us
  Pallas kernels  129 us (98%)
  local copies, waits for them, and re-layouts  3.01 us (2%)
    pallas_call x1, Pallas kernels, local(): pl.pallas_call(kernel, out_shape=jax.ShapeDtypeStruct((4, 64, 256), F32),...  129 us

profile of v1, /device:TPU:0, one launch (start us, length us, event | category | flops | bytes accessed | tf_op | source)
XLA Modules:
  0.0 131.8 jit_solution(10201291692233137066)
XLA Ops:
  0.0 1.3 %copy.5.blocks = s32[4,2]{1,0:T(4,128)} copy(s32[4,2]{0,1:T(2,128)} %bitcast.6) | data formatting | bytes 64 | tf_op jit(solution)/shard_map/reshape | solution.py:395
  1.3 128.7 %shard_map.46 = f32[4,64,256]{2,1,0:T(8,128)} custom-call(s32[4,2]{1,0:T(4,128)} %copy.5.blocks, s32[4]{0:T(128)} %bitcast.7, f32[4096,256]{1,0:T(8,128)} %x_ref.1, f32[4,4,4,64,256]{4,3,2,1,0:T(8,128)} %bitcast.4), custom_call_target="tpu_custom_call" | custom-call | tf_op jit(solution)/shard_map/pallas_call | solution.py:358
  130.1 1.7 %copy.7 = f32[256,256]{1,0:T(8,128)} copy(f32[256,256]{1,0:T(8,128)} %bitcast.5) | data formatting | bytes 524288

commit v2 on v1

v2 whole, which is shorter than its diff:
```python
import functools
import math

import jax
import jax.numpy as jnp
from jax import lax
from jax.experimental import pallas as pl
from jax.experimental.pallas import tpu as pltpu
from jax.sharding import PartitionSpec as P

MESH = pl.DeviceIdType.MESH
LOG2E = 1.0 / math.log(2.0)
EPS = math.exp(-3.0)
F32 = jnp.float32
BF16 = jnp.bfloat16
MCH = 1024
NT = (((1,), (1,)), ((), ()))


def split(v):
    hi = v.astype(BF16)
    return hi, (v - hi.astype(F32)).astype(BF16)


def repeat8(a):
    return jnp.concatenate([a] * 8, axis=1)


def spread(v):
    return jnp.broadcast_to(v, (128, 128)).T


def wait_bytes(ref, sem):
    pltpu.make_async_copy(ref, ref, sem).wait()


def kernel(
    blocks, counts, x_hbm, c_hbm, out_ref,
    e, s, ccat, xcat, bias, arep, raw0, raw1, cown,
    rg0, rg, alpha, gvec, dg, mg, mrep, y1, z1, u0, u1,
    c_sem, r_send, r_recv, d_send, d_recv, m_send, m_recv, p_send, p_recv,
):
    dp = lax.axis_index("dp")
    code = lax.axis_index("code")
    z, y = dp // 4, dp % 4
    raws = (raw0, raw1)

    def code_peer(d):
        return (dp, (code + d) % 8)

    def dp_peer(d):
        return ((dp + d) % 16, code)

    def z_peer(d):
        return (((z + d) % 4) * 4 + y, code)

    def y_peer(d):
        return (z * 4 + (y + d) % 4, code)

    def push(src, dst, send, recv, peer):
        pltpu.make_async_remote_copy(
            src_ref=src, dst_ref=dst, send_sem=send, recv_sem=recv,
            device_id=peer, device_id_type=MESH,
        ).start()

    for h in range(2):
        for p in range(4):
            for q in range(4):
                pltpu.make_async_copy(
                    c_hbm.at[:, q, p, :, pl.ds(h * 128, 128)],
                    s.at[h, :, p, pl.ds(q * 64, 64), :],
                    c_sem.at[0],
                ).start()
    for r in range(4):
        pltpu.make_async_copy(x_hbm.at[r], e.at[7, :, pl.ds(r * 256, 256)], c_sem.at[1]).start()
    own_copy = pltpu.make_async_copy(c_hbm.at[z, y], cown, c_sem.at[2])
    own_copy.start()

    barrier = pltpu.get_barrier_semaphore()
    for d in range(1, 8):
        pl.semaphore_signal(barrier, inc=1, device_id=code_peer(d), device_id_type=MESH)
    for d in range(1, 16):
        pl.semaphore_signal(barrier, inc=1, device_id=dp_peer(d), device_id_type=MESH)

    wait_bytes(s, c_sem.at[0])

    def prepare(n, carry):
        b, p = n // 4, n % 4
        c0 = s[0, b, p]
        c1 = s[1, b, p]
        norm = jnp.sum(c0 * c0 + c1 * c1, axis=1, keepdims=True) * (-0.25 * LOG2E)
        rows = pl.ds(pl.multiple_of(p * 256, 256), 256)
        bias[b, rows, :] = jnp.broadcast_to(norm, (256, 128))
        for h, part in enumerate((c0, c1)):
            hi, lo = split(part * (0.5 * LOG2E))
            ccat[b, rows, h * 128:(h + 1) * 128] = hi
            ccat[b, rows, 256 + h * 128:256 + (h + 1) * 128] = lo
        return carry

    lax.fori_loop(0, 16, prepare, 0)
    wait_bytes(e.at[7], c_sem.at[1])

    def score(r, iq):
        raw = raws[iq % 2]
        lanes = slice(iq * 256, (iq + 1) * 256)
        xs = e[7, lanes, pl.ds(pl.multiple_of(r * 256, 256), 256)]
        xh, xl = split(xs)
        xcat[r, lanes, 0:256] = xh
        xcat[r, lanes, 256:512] = xl
        rhs = jnp.concatenate([xh, xl, xh], axis=1)
        top = None
        for slot in range(2):
            b = blocks[r, 0, slot]
            peak = None
            for k in range(0, 1024, MCH):
                rows = slice(k, k + MCH)
                ch = ccat[b, rows, 0:256]
                cl = ccat[b, rows, 256:512]
                lhs = jnp.concatenate([ch, ch, cl], axis=1)
                bb = bias[b, rows, :]
                value = lax.dot_general(lhs, rhs, NT, preferred_element_type=F32)
                value = value + jnp.concatenate([bb, bb], axis=1)
                raw[slot * 4 + k // 256:slot * 4 + (k + MCH) // 256] = value.reshape(MCH // 256, 256, 256)
                peak_k = jnp.max(value.reshape(MCH // 8, 8, 256), axis=0)
                peak = peak_k if peak is None else jnp.maximum(peak, peak_k)
            peak = jnp.max(peak, axis=0, keepdims=True)
            if slot == 0:
                top = peak
            else:
                top = jnp.where(counts[r, 0] > 1, jnp.maximum(top, peak), top)
        rg0[r, code, :, lanes] = top

    def expo(r, iq):
        raw = raws[iq % 2]
        lanes = slice(iq * 256, (iq + 1) * 256)
        top = rg0[r, code, :, lanes]
        total = jnp.zeros((8, 256), F32)
        for slot in range(2):
            shift = top if slot == 0 else jnp.where(counts[r, 0] > 1, top, 3e38)
            for k in range(0, 1024, 256):
                rows = slice(k, k + 256)
                w = jnp.exp2(raw[slot * 4 + k // 256] - shift)
                e[r * 2 + slot, rows, lanes] = w
                total = total + jnp.sum(w.reshape(32, 8, 256), axis=0)
        rg0[r, code, :, 1024 + iq * 256:1280 + iq * 256] = jnp.sum(total, axis=0, keepdims=True)

    def send_first(r):
        for d in range(1, 8):
            push(rg0.at[r, code], rg0.at[r, code], r_send.at[0, r], r_recv.at[0, r], code_peer(d))

    score(0, 0)

    def row_first(r, carry):
        for iq in range(3):
            score(r, iq + 1)
            expo(r, iq)

        @pl.when(r == 0)
        def _():
            pl.semaphore_wait(barrier, 22)

        score(r + 1, 0)
        expo(r, 3)
        send_first(r)
        return carry

    lax.fori_loop(0, 3, row_first, 0)
    for iq in range(3):
        score(3, iq + 1)
        expo(3, iq)
    expo(3, 3)
    send_first(3)

    def col_block(r):
        g = gvec[r]
        for slot in range(2):
            def chunk(n, carry):
                k = pl.ds(pl.multiple_of(n * 256, 256), 256)
                w = e[r * 2 + slot, k, :] * g
                acc = w[:, 0:128]
                for j in range(1, 8):
                    acc = acc + w[:, j * 128:(j + 1) * 128]
                s[r // 2, (r % 2) * 2 + slot, n] = acc
                return carry

            lax.fori_loop(0, 4, chunk, 0)

    def col_first(r, carry):
        wait_bytes(rg0.at[r, pl.ds(0, 7)], r_recv.at[0, r])
        tops = [rg0[r, j, :, 0:1024] for j in range(8)]
        best = functools.reduce(jnp.maximum, tops)
        total = jnp.zeros((1, 1024), F32)
        for j in range(8):
            total = total + jnp.exp2(tops[j] - best) * rg0[r, j, :, 1024:2048]
        mine = jnp.exp2(rg0[r, code, :, 0:1024] - best)
        alpha[r] = mine
        gvec[r] = mine / total
        col_block(r)
        return carry

    def factor(it, r):
        wait_bytes(rg.at[it, r, pl.ds(0, 7)], r_recv.at[it + 1, r])
        total = rg[it, r, 0]
        for j in range(1, 8):
            total = total + rg[it, r, j]
        gvec[r] = alpha[r] / total

    def col_next(r, carry):
        factor(0, r)
        col_block(r)
        return carry

    def row_next(it):
        def body(r, carry):
            acc = jnp.zeros((8, 1024), F32)
            for slot in range(2):
                b = blocks[r, 0, slot]

                def chunk(n, acc):
                    k = pl.ds(pl.multiple_of(n * 64, 64), 64)
                    w = e[r * 2 + slot, k, :] * repeat8(arep[b, k, :])
                    return acc + jnp.sum(w.reshape(8, 8, 1024), axis=0)

                acc = lax.fori_loop(0, 16, chunk, acc)
            rg[it, r, code] = jnp.sum(acc, axis=0, keepdims=True) * alpha[r]
            for d in range(1, 8):
                push(
                    rg.at[it, r, code], rg.at[it, r, code],
                    r_send.at[it + 1, r], r_recv.at[it + 1, r], code_peer(d),
                )
            return carry

        return body

    def has_slot(r, b):
        second = (blocks[r, 0, 1] == b) & (counts[r, 0] > 1)
        slot = jnp.where(second, 1, 0)
        has = second | (blocks[r, 0, 0] == b)
        return has, slot

    def next_a(it):
        def gather(b, carry):
            for p in range(4):
                total = jnp.zeros((256, 128), F32)
                for r in range(4):
                    has, slot = has_slot(r, b)
                    total = total + jnp.where(has, s[r // 2, (r % 2) * 2 + slot, p], 0.0)
                for j in range(2):
                    row = jnp.sum(total[j * 128:(j + 1) * 128, :].T, axis=0, keepdims=True)
                    dg[it, dp, pl.ds(b * 8 + p * 2 + j, 1), :] = row
            return carry

        lax.fori_loop(0, 4, gather, 0)
        for d in range(1, 16):
            push(dg.at[it, dp], dg.at[it, dp], d_send.at[it], d_recv.at[it], dp_peer(d))
        wait_bytes(dg.at[it, pl.ds(0, 15)], d_recv.at[it])
        total = dg[it, 0]
        for j in range(1, 16):
            total = total + dg[it, j]
        mrep[0, 0:32, :] = 1.0 / (total + EPS)

        def lay(b, carry):
            for j in range(8):
                arep[b, j * 128:(j + 1) * 128, :] = spread(mrep[0, pl.ds(b * 8 + j, 1), :])
            return carry

        lax.fori_loop(0, 4, lay, 0)

    lax.fori_loop(0, 4, col_first, 0)
    next_a(0)
    lax.fori_loop(0, 4, row_next(0), 0)
    lax.fori_loop(0, 4, col_next, 0)
    next_a(1)
    lax.fori_loop(0, 4, row_next(1), 0)

    def last_factor(r, carry):
        factor(1, r)
        return carry

    lax.fori_loop(0, 4, last_factor, 0)

    def reduce_first(p):
        wait_bytes(y1.at[:, p], p_recv.at[0, p])
        wait_bytes(z1.at[:, p], p_recv.at[1, p])
        own = pl.ds(pl.multiple_of(y * 64, 64), 64)
        for b in range(4):
            s[0, b, p, own, :] = (s[0, b, p, own, :] + y1[0, p, b]) + (y1[1, p, b] + y1[2, p, b])
        s[1, z, p] = (s[1, z, p] + z1[0, p]) + (z1[1, p] + z1[2, p])
        for d in range(1, 4):
            push(s.at[0, (z + d) % 4, p, own, :], u0.at[d - 1, p], p_send.at[2, p], p_recv.at[2, p], z_peer(d))
            dest = pl.ds(pl.multiple_of(((y + d) % 4) * 64, 64), 64)
            push(s.at[1, z, p, dest, :], u1.at[d - 1, p], p_send.at[3, p], p_recv.at[3, p], y_peer(d))

    def part(p, carry):
        rows = pl.ds(pl.multiple_of(p * 256, 256), 256)

        def one(r, carry):
            xh = xcat[r, :, 0:256]
            xl = xcat[r, :, 256:512]
            rhs = jnp.concatenate([xh, xl, xh], axis=0)
            g = gvec[r]
            for slot in range(2):
                w = e[r * 2 + slot, rows, :] * g
                acc = w[:, 0:128]
                for j in range(1, 8):
                    acc = acc + w[:, j * 128:(j + 1) * 128]
                t = r * 2 + slot
                raw1[t, :, 0:128] = acc
                eh, el = split(w)
                lhs = jnp.concatenate([eh, eh, el], axis=1)
                raw0[t] = jnp.dot(lhs, rhs, preferred_element_type=F32)
            return carry

        lax.fori_loop(0, 4, one, 0)
        for b in range(4):
            total = jnp.zeros((256, 256), F32)
            mass = jnp.zeros((256, 128), F32)
            for r in range(4):
                has, slot = has_slot(r, b)
                total = total + jnp.where(has, raw0[r * 2 + slot], 0.0)
                mass = mass + jnp.where(has, raw1[r * 2 + slot, :, 0:128], 0.0)
            s[0, b, p] = total[:, 0:128]
            s[1, b, p] = total[:, 128:256]
            for j in range(2):
                mg[p, dp, b * 2 + j:b * 2 + j + 1, :] = jnp.sum(
                    mass[j * 128:(j + 1) * 128, :].T, axis=0, keepdims=True
                )
        for d in range(1, 4):
            dest = pl.ds(pl.multiple_of(((y + d) % 4) * 64, 64), 64)
            push(s.at[0, :, p, dest, :], y1.at[d - 1, p], p_send.at[0, p], p_recv.at[0, p], y_peer(d))
            push(s.at[1, (z + d) % 4, p], z1.at[d - 1, p], p_send.at[1, p], p_recv.at[1, p], z_peer(d))
        for d in range(1, 16):
            push(mg.at[p, dp], mg.at[p, dp], m_send.at[p], m_recv.at[p], dp_peer(d))

        @pl.when(p > 0)
        def _():
            reduce_first(p - 1)

        return carry

    lax.fori_loop(0, 4, part, 0)
    own_copy.wait()
    reduce_first(3)

    def finish(p, carry):
        wait_bytes(mg.at[p, pl.ds(0, 15)], m_recv.at[p])
        mass = mg[p, 0]
        for j in range(1, 16):
            mass = mass + mg[p, j]
        mrep[1, 0:8, :] = 1.0 / (mass + EPS)
        mrep[0] = spread(mrep[1, pl.ds(z * 2 + y // 2, 1), :])
        a = mrep[0, pl.ds(pl.multiple_of((y % 2) * 64, 64), 64), :]
        wait_bytes(u0.at[:, p], p_recv.at[2, p])
        wait_bytes(u1.at[:, p], p_recv.at[3, p])
        own = pl.ds(pl.multiple_of(y * 64, 64), 64)
        f0 = (s[0, z, p, own, :] + u0[0, p]) + (u0[1, p] + u0[2, p])
        f1 = (s[1, z, p, own, :] + u1[0, p]) + (u1[1, p] + u1[2, p])
        out_ref[p, :, 0:128] = (f0 + EPS * cown[p, :, 0:128]) * a
        out_ref[p, :, 128:256] = (f1 + EPS * cown[p, :, 128:256]) * a
        return carry

    lax.fori_loop(0, 4, finish, 0)

    def drain_rows(r, carry):
        wait_bytes(rg0.at[r, pl.ds(0, 7)], r_send.at[0, r])
        wait_bytes(rg.at[0, r, pl.ds(0, 7)], r_send.at[1, r])
        wait_bytes(rg.at[1, r, pl.ds(0, 7)], r_send.at[2, r])
        wait_bytes(mg.at[r, pl.ds(0, 15)], m_send.at[r])
        wait_bytes(y1.at[:, r], p_send.at[0, r])
        wait_bytes(z1.at[:, r], p_send.at[1, r])
        wait_bytes(u0.at[:, r], p_send.at[2, r])
        wait_bytes(u1.at[:, r], p_send.at[3, r])
        return carry

    lax.fori_loop(0, 4, drain_rows, 0)
    for it in range(2):
        wait_bytes(dg.at[it, pl.ds(0, 15)], d_send.at[it])


def local(vectors, codebook, cand_blocks, cand_counts):
    smem = pl.BlockSpec(memory_space=pltpu.SMEM)
    hbm = pl.BlockSpec(memory_space=pl.ANY)
    out = pl.pallas_call(
        kernel,
        out_shape=jax.ShapeDtypeStruct((4, 64, 256), F32),
        in_specs=[smem, smem, hbm, hbm],
        out_specs=pl.BlockSpec(memory_space=pltpu.VMEM),
        scratch_shapes=[
            pltpu.VMEM((8, 1024, 1024), F32),
            pltpu.VMEM((2, 4, 4, 256, 128), F32),
            pltpu.VMEM((4, 1024, 512), BF16),
            pltpu.VMEM((4, 1024, 512), BF16),
            pltpu.VMEM((4, 1024, 128), F32),
            pltpu.VMEM((4, 1024, 128), F32),
            pltpu.VMEM((8, 256, 256), F32),
            pltpu.VMEM((8, 256, 256), F32),
            pltpu.VMEM((4, 64, 256), F32),
            pltpu.VMEM((4, 8, 1, 2048), F32),
            pltpu.VMEM((2, 4, 8, 1, 1024), F32),
            pltpu.VMEM((4, 1, 1024), F32),
            pltpu.VMEM((4, 1, 1024), F32),
            pltpu.VMEM((2, 16, 32, 128), F32),
            pltpu.VMEM((4, 16, 8, 128), F32),
            pltpu.VMEM((2, 128, 128), F32),
            pltpu.VMEM((3, 4, 4, 64, 128), F32),
            pltpu.VMEM((3, 4, 256, 128), F32),
            pltpu.VMEM((3, 4, 64, 128), F32),
            pltpu.VMEM((3, 4, 64, 128), F32),
            pltpu.SemaphoreType.DMA((3,)),
            pltpu.SemaphoreType.DMA((3, 4)),
            pltpu.SemaphoreType.DMA((3, 4)),
            pltpu.SemaphoreType.DMA((2,)),
            pltpu.SemaphoreType.DMA((2,)),
            pltpu.SemaphoreType.DMA((4,)),
            pltpu.SemaphoreType.DMA((4,)),
            pltpu.SemaphoreType.DMA((4, 4)),
            pltpu.SemaphoreType.DMA((4, 4)),
        ],
        compiler_params=pltpu.CompilerParams(
            collective_id=0, has_side_effects=True, vmem_limit_bytes=63 * 1024 * 1024,
        ),
    )(
        cand_blocks,
        cand_counts,
        vectors.reshape(4, 1024, 256),
        codebook.reshape(4, 4, 4, 64, 256),
    )
    return out.reshape(256, 256)


def solution(mesh):
    return jax.shard_map(
        local,
        mesh=mesh,
        in_specs=(P("dp", None), P("code", None), P("dp", "code", None), P("dp", "code")),
        out_specs=P(("code", "dp"), None),
        check_vma=False,
    )
```

time: 132 us -> 108 us (0.82)
  Pallas kernels: 129 us -> 104 us
    pallas_call x1, Pallas kernels: 129 us -> 104 us  [local(): pl.pallas_call(kernel, out_shape=jax.ShapeDtypeStruct((4, 64, 256), F32),...]
    unnamed x1 -> x3, local copies, waits for them, and re-layouts: 1.67 us -> 4.31 us
    reshape x1 -> x0, local copies, waits for them, and re-layouts: 1.34 us -> none  [local(): cand_blocks.reshape(4, 2)]
where the time goes in v2:
time: 108 us
  Pallas kernels  104 us (96%)
  local copies, waits for them, and re-layouts  4.31 us (4%)
    pallas_call x1, Pallas kernels, local(): pl.pallas_call(kernel, out_shape=jax.ShapeDtypeStruct((4, 64, 256), F32),...  104 us
    unnamed x3, local copies, waits for them, and re-layouts  4.31 us

profile of v2, /device:TPU:0, one launch (start us, length us, event | category | flops | bytes accessed | tf_op | source)
XLA Modules:
  0.0 107.8 jit_solution(16095130900708264828)
XLA Ops:
  0.0 1.3 %copy.5.blocks = s32[4,1,2]{2,1,0:T(1,128)} copy(s32[4,1,2]{0,2,1:T(2,128)} %param.6) | data formatting | bytes 64 | tf_op args[2]
  1.3 1.3 %copy.6.counts = s32[4,1]{1,0:T(4,128)} copy(s32[4,1]{0,1:T(1,128)} %param.7) | data formatting | bytes 32 | tf_op args[3]
  2.6 103.5 %shard_map.46 = f32[4,64,256]{2,1,0:T(8,128)} custom-call(s32[4,1,2]{2,1,0:T(1,128)} %copy.5.blocks, s32[4,1]{1,0:T(4,128)} %copy.6.counts, f32[4,1024,256]{2,1,0:T(8,128)} %bitcast.3, f32[4,4,4,64,256]{4,3,2,1,0:T(8,128)} %bitcast.4), custom_call_target="tpu_custom_call" | custom-call | tf_op jit(solution)/shard_map/pallas_call | solution.py:383
  106.2 1.7 %copy.8 = f32[256,256]{1,0:T(8,128)} copy(f32[256,256]{1,0:T(8,128)} %bitcast.5) | data formatting | bytes 524288

commit v3 on v2

v3 whole, which is shorter than its diff:
```python
import functools
import math

import jax
import jax.numpy as jnp
from jax import lax
from jax.experimental import pallas as pl
from jax.experimental.pallas import tpu as pltpu
from jax.sharding import PartitionSpec as P

MESH = pl.DeviceIdType.MESH
LOG2E = 1.0 / math.log(2.0)
EPS = math.exp(-3.0)
F32 = jnp.float32
BF16 = jnp.bfloat16
F8 = jnp.float8_e5m2
NP = 8
CH = 1024 // NP
Q = CH // 4
LAG1 = 2
LAG2 = 6
LAG3 = 9
DIRECT = 1
NT = (((1,), (1,)), ((), ()))


def split(v):
    hi = v.astype(BF16)
    return hi, (v - hi.astype(F32)).astype(BF16)


def repeat8(a):
    return jnp.concatenate([a] * 8, axis=1)


def spread(v):
    return jnp.broadcast_to(v, (128, 128)).T


def wait_bytes(ref, sem):
    pltpu.make_async_copy(ref, ref, sem).wait()


def kernel(
    blocks, counts, x_hbm, c_hbm, out_ref,
    e, s, ccat, xcat, x8, bias, arep, raw0, raw1, cown,
    rg0, rg, alpha, gvec, dg, my, mz, mrep, ya, yb, yc, yd, za, zb, zc, zd, u0, u1,
    c_sem, r_send, r_recv, d_send, d_recv, m_send, m_recv, p_send, p_recv,
):
    dp = lax.axis_index("dp")
    code = lax.axis_index("code")
    z, y = dp // 4, dp % 4
    raws = (raw0, raw1)

    code_peers = [(dp, (code + d) % 8) for d in range(8)]
    dp_peers = [((dp + d) % 16, code) for d in range(16)]

    def z_peer(d):
        return (((z + d) % 4) * 4 + y, code)

    def y_peer(d):
        return (z * 4 + (y + d) % 4, code)

    def push(src, dst, send, recv, peer):
        pltpu.make_async_remote_copy(
            src_ref=src, dst_ref=dst, send_sem=send, recv_sem=recv,
            device_id=peer, device_id_type=MESH,
        ).start()

    for h in range(2):
        for p in range(NP):
            pltpu.make_async_copy(
                c_hbm.at[:, :, p, :, pl.ds(h * 128, 128)], s.at[h, :, p], c_sem.at[0]
            ).start()
    for r in range(4):
        pltpu.make_async_copy(x_hbm.at[r], e.at[7, :, pl.ds(r * 256, 256)], c_sem.at[1]).start()
    own_copy = pltpu.make_async_copy(c_hbm.at[z, y], cown, c_sem.at[2])
    own_copy.start()

    barrier = pltpu.get_barrier_semaphore()
    for d in range(1, 8):
        pl.semaphore_signal(barrier, inc=1, device_id=code_peers[d], device_id_type=MESH)
    for d in range(1, 16):
        pl.semaphore_signal(barrier, inc=1, device_id=dp_peers[d], device_id_type=MESH)

    wait_bytes(s, c_sem.at[0])

    def prepare(n, carry):
        b, p = n // NP, n % NP
        c0 = s[0, b, p].reshape(CH, 128)
        c1 = s[1, b, p].reshape(CH, 128)
        norm = jnp.sum(c0 * c0 + c1 * c1, axis=1, keepdims=True) * (-0.25 * LOG2E)
        rows = pl.ds(pl.multiple_of(p * CH, CH), CH)
        bias[b, rows, :] = jnp.broadcast_to(norm, (CH, 128))
        for h, part in enumerate((c0, c1)):
            hi, lo = split(part * (0.5 * LOG2E))
            ccat[b, rows, h * 128:(h + 1) * 128] = hi
            ccat[b, rows, 256 + h * 128:256 + (h + 1) * 128] = lo
        return carry

    lax.fori_loop(0, 4 * NP, prepare, 0)
    wait_bytes(e.at[7], c_sem.at[1])

    def score(r, iq):
        raw = raws[iq % 2]
        lanes = slice(iq * 256, (iq + 1) * 256)
        xs = e[7, lanes, pl.ds(pl.multiple_of(r * 256, 256), 256)]
        xh, xl = split(xs)
        xcat[r, lanes, 0:256] = xh
        x8[r, lanes, :] = ((xs - xh.astype(F32)) * 256.0).astype(F8)
        x8[r, iq * 256 + 1024:iq * 256 + 1280, :] = xs.astype(F8)
        rhs = jnp.concatenate([xh, xl, xh], axis=1)
        top = None
        for slot in range(2):
            b = blocks[r, 0, slot]
            ch = ccat[b, :, 0:256]
            cl = ccat[b, :, 256:512]
            lhs = jnp.concatenate([ch, ch, cl], axis=1)
            bb = bias[b]
            value = lax.dot_general(lhs, rhs, NT, preferred_element_type=F32)
            value = value + jnp.concatenate([bb, bb], axis=1)
            raw[slot * 4:slot * 4 + 4] = value.reshape(4, 256, 256)
            peak = jnp.max(value.reshape(128, 8, 256), axis=0)
            peak = jnp.max(peak, axis=0, keepdims=True)
            if slot == 0:
                top = peak
            else:
                top = jnp.where(counts[r, 0] > 1, jnp.maximum(top, peak), top)
        rg0[r, code, :, lanes] = top

    def expo(r, iq):
        raw = raws[iq % 2]
        lanes = slice(iq * 256, (iq + 1) * 256)
        top = rg0[r, code, :, lanes]
        total = jnp.zeros((8, 256), F32)
        for slot in range(2):
            shift = top if slot == 0 else jnp.where(counts[r, 0] > 1, top, 3e38)
            for k in range(0, 1024, 256):
                rows = slice(k, k + 256)
                w = jnp.exp2(raw[slot * 4 + k // 256] - shift)
                e[r * 2 + slot, rows, lanes] = w
                total = total + jnp.sum(w.reshape(32, 8, 256), axis=0)
        rg0[r, code, :, 1024 + iq * 256:1280 + iq * 256] = jnp.sum(total, axis=0, keepdims=True)

    def send_first(r):
        for d in range(1, 8):
            push(rg0.at[r, code], rg0.at[r, code], r_send.at[0, r], r_recv.at[0, r], code_peers[d])

    score(0, 0)

    def row_first(r, carry):
        for iq in range(3):
            score(r, iq + 1)
            expo(r, iq)

        @pl.when(r == 0)
        def _():
            pl.semaphore_wait(barrier, 22)

        score(r + 1, 0)
        expo(r, 3)
        send_first(r)
        return carry

    lax.fori_loop(0, 3, row_first, 0)
    for iq in range(3):
        score(3, iq + 1)
        expo(3, iq)
    expo(3, 3)
    send_first(3)

    def col_block(r):
        g = gvec[r]
        for slot in range(2):
            def chunk(n, carry):
                k = pl.ds(pl.multiple_of(n * 256, 256), 256)
                w = e[r * 2 + slot, k, :] * g
                acc = w[:, 0:128]
                for j in range(1, 8):
                    acc = acc + w[:, j * 128:(j + 1) * 128]
                s[r // 2, (r % 2) * 2 + slot, pl.ds(n * 2, 2)] = acc.reshape(2, 4, Q, 128)
                return carry

            lax.fori_loop(0, 4, chunk, 0)

    def col_first(r, carry):
        wait_bytes(rg0.at[r, pl.ds(0, 7)], r_recv.at[0, r])
        tops = [rg0[r, j, :, 0:1024] for j in range(8)]
        best = functools.reduce(jnp.maximum, tops)
        total = jnp.zeros((1, 1024), F32)
        for j in range(8):
            total = total + jnp.exp2(tops[j] - best) * rg0[r, j, :, 1024:2048]
        mine = jnp.exp2(rg0[r, code, :, 0:1024] - best)
        alpha[r] = mine
        gvec[r] = mine / total
        col_block(r)
        return carry

    def factor(it, r):
        wait_bytes(rg.at[it, r, pl.ds(0, 7)], r_recv.at[it + 1, r])
        total = rg[it, r, 0]
        for j in range(1, 8):
            total = total + rg[it, r, j]
        gvec[r] = alpha[r] / total

    def col_next(r, carry):
        factor(0, r)
        col_block(r)
        return carry

    def row_next(it):
        def body(r, carry):
            acc = jnp.zeros((8, 1024), F32)
            for slot in range(2):
                b = blocks[r, 0, slot]

                def chunk(n, acc):
                    k = pl.ds(pl.multiple_of(n * 256, 256), 256)
                    w = e[r * 2 + slot, k, :] * repeat8(arep[b, k, :])
                    return acc + jnp.sum(w.reshape(32, 8, 1024), axis=0)

                acc = lax.fori_loop(0, 4, chunk, acc)
            rg[it, r, code] = jnp.sum(acc, axis=0, keepdims=True) * alpha[r]
            for d in range(1, 8):
                push(
                    rg.at[it, r, code], rg.at[it, r, code],
                    r_send.at[it + 1, r], r_recv.at[it + 1, r], code_peers[d],
                )
            return carry

        return body

    def has_slot(r, b):
        second = (blocks[r, 0, 1] == b) & (counts[r, 0] > 1)
        slot = jnp.where(second, 1, 0)
        has = second | (blocks[r, 0, 0] == b)
        return has, slot

    def next_a(it):
        def gather(b, carry):
            for p in range(NP):
                total = jnp.zeros((4, Q, 128), F32)
                for r in range(4):
                    has, slot = has_slot(r, b)
                    total = total + jnp.where(has, s[r // 2, (r % 2) * 2 + slot, p], 0.0)
                row = jnp.sum(total.reshape(128, 128).T, axis=0, keepdims=True)
                dg[it, b, dp, p:p + 1, :] = row
            for d in range(1, 16):
                push(dg.at[it, b, dp], dg.at[it, b, dp], d_send.at[it, b], d_recv.at[it, b], dp_peers[d])
            return carry

        lax.fori_loop(0, 4, gather, 0)

        def lay(b, carry):
            wait_bytes(dg.at[it, b, pl.ds(0, 15)], d_recv.at[it, b])
            parts = [dg[it, b, j] for j in range(16)]
            while len(parts) > 1:
                parts = [parts[j] + parts[j + 1] for j in range(0, len(parts), 2)]
            a = 1.0 / (parts[0] + EPS)
            for j in range(8):
                arep[b, j * 128:(j + 1) * 128, :] = spread(a[j:j + 1, :])
            return carry

        lax.fori_loop(0, 4, lay, 0)

    lax.fori_loop(0, 4, col_first, 0)
    next_a(0)
    lax.fori_loop(0, 4, row_next(0), 0)
    lax.fori_loop(0, 4, col_next, 0)
    next_a(1)
    lax.fori_loop(0, 4, row_next(1), 0)

    def last_factor(r, carry):
        factor(1, r)
        return carry

    lax.fori_loop(0, 4, last_factor, 0)

    def part(p):
        rows = pl.ds(pl.multiple_of(p * CH, CH), CH)

        def one(r, carry):
            xh = xcat[r, :, 0:256]
            g = gvec[r]
            parts = []
            for slot in range(2):
                w = (e[r * 2 + slot, rows, :] * g) * repeat8(arep[blocks[r, 0, slot], rows, :])
                acc = w[:, 0:128]
                for j in range(1, 8):
                    acc = acc + w[:, j * 128:(j + 1) * 128]
                raw1[r * 2 + slot, 0:CH, 0:128] = acc
                hi = w.astype(BF16)
                lo = w - hi.astype(F32)
                parts.append((hi, jnp.concatenate([(w * 2.0**15).astype(F8), (lo * 2.0**23).astype(F8)], axis=1)))
            eh = jnp.concatenate([hi for hi, lo in parts], axis=0)
            el = jnp.concatenate([lo for hi, lo in parts], axis=0)
            value = jnp.dot(eh, xh, preferred_element_type=F32)
            value = value + jnp.dot(el, x8[r], preferred_element_type=F32) * 2.0**-23
            for slot in range(2):
                raw0[r * 2 + slot, 0:CH, :] = value[slot * CH:(slot + 1) * CH]
            return carry

        lax.fori_loop(0, 4, one, 0)
        for b in range(4):
            total = jnp.zeros((CH, 256), F32)
            mass = jnp.zeros((CH, 128), F32)
            for r in range(4):
                has, slot = has_slot(r, b)
                total = total + jnp.where(has, raw0[r * 2 + slot, 0:CH, :], 0.0)
                mass = mass + jnp.where(has, raw1[r * 2 + slot, 0:CH, 0:128], 0.0)
            s[0, b, p] = total[:, 0:128].reshape(4, Q, 128)
            s[1, b, p] = total[:, 128:256].reshape(4, Q, 128)
            my[p // 2, y, pl.ds((p % 2) * 4 + b, 1), :] = jnp.sum(mass.T, axis=0, keepdims=True)

    y_next, y_last, y_far = (y + 1) % 4, (y + 3) % 4, (y + 2) % 4
    z_next, z_last, z_far = (z + 1) % 4, (z + 3) % 4, (z + 2) % 4
    to_y_next, to_y_last = y_peer(1), y_peer(3)
    to_z_next, to_z_last = z_peer(1), z_peer(3)

    def far_parts(p, peers):
        push(s.at[0, pl.ds(0, 2), p, y_far], ya.at[p], p_send.at[0, p], p_recv.at[0, p], peers[0])
        push(s.at[1, z_far, p, pl.ds(0, 2)], za.at[p], p_send.at[2, p], p_recv.at[2, p], peers[1])
        push(s.at[0, pl.ds(2, 2), p, y_far], yb.at[p], p_send.at[1, p], p_recv.at[1, p], peers[2])
        push(s.at[1, z_far, p, pl.ds(2, 2)], zb.at[p], p_send.at[3, p], p_recv.at[3, p], peers[3])

    def next_y(p):
        push(s.at[0, :, p, y_next], yc.at[p], p_send.at[4, p], p_recv.at[4, p], to_y_next)

    def next_z(p):
        push(s.at[1, z_next, p], zc.at[p], p_send.at[6, p], p_recv.at[6, p], to_z_next)

    def last_y(p):
        push(s.at[0, :, p, y_last], yd.at[p], p_send.at[5, p], p_recv.at[5, p], to_y_last)

    def last_z(p):
        push(s.at[1, z_last, p], zd.at[p], p_send.at[7, p], p_recv.at[7, p], to_z_last)

    def step_one(p):
        @pl.when(p < NP - DIRECT)
        def _():
            far_parts(p, (to_y_next, to_z_next, to_y_last, to_z_last))

        @pl.when(p >= NP - DIRECT)
        def _():
            far_parts(p, (y_peer(2), z_peer(2), y_peer(2), z_peer(2)))
            next_y(p)
            next_z(p)
            last_y(p)
            last_z(p)

        @pl.when(p % 2 == 1)
        def _():
            for d in range(1, 4):
                push(my.at[p // 2, y], my.at[p // 2, y], m_send.at[0, p // 2], m_recv.at[0, p // 2], y_peer(d))

    def step_two(p):
        wait_bytes(ya.at[p], p_recv.at[0, p])
        s[0, 0:2, p, y_next] = s[0, 0:2, p, y_next] + ya[p]
        next_y(p)
        wait_bytes(za.at[p], p_recv.at[2, p])
        s[1, z_next, p, 0:2] = s[1, z_next, p, 0:2] + za[p]
        next_z(p)
        wait_bytes(yb.at[p], p_recv.at[1, p])
        s[0, 2:4, p, y_last] = s[0, 2:4, p, y_last] + yb[p]
        last_y(p)
        wait_bytes(zb.at[p], p_recv.at[3, p])
        s[1, z_last, p, 2:4] = s[1, z_last, p, 2:4] + zb[p]
        last_z(p)

    def step_three(p):
        wait_bytes(yc.at[p], p_recv.at[4, p])
        wait_bytes(yd.at[p], p_recv.at[5, p])

        @pl.when(p >= NP - DIRECT)
        def _():
            for n, ref in enumerate((ya, yb, za, zb)):
                wait_bytes(ref.at[p], p_recv.at[n, p])
            s[0, 0:2, p, y] = s[0, 0:2, p, y] + ya[p]
            s[0, 2:4, p, y] = s[0, 2:4, p, y] + yb[p]
            s[1, z, p, 0:2] = s[1, z, p, 0:2] + za[p]
            s[1, z, p, 2:4] = s[1, z, p, 2:4] + zb[p]

        s[0, :, p, y] = (s[0, :, p, y] + yc[p]) + yd[p]
        for d in range(1, 4):
            push(s.at[0, (z + d) % 4, p, y], u0.at[d - 1, p], p_send.at[8, p], p_recv.at[8, p], z_peer(d))
        wait_bytes(zc.at[p], p_recv.at[6, p])
        wait_bytes(zd.at[p], p_recv.at[7, p])
        s[1, z, p] = (s[1, z, p] + zc[p]) + zd[p]
        for d in range(1, 4):
            push(s.at[1, z, p, (y + d) % 4], u1.at[d - 1, p], p_send.at[9, p], p_recv.at[9, p], y_peer(d))

        @pl.when(p % 2 == 1)
        def _():
            n = p // 2
            wait_bytes(my.at[n, pl.ds(0, 3)], m_recv.at[0, n])
            mz[n, z] = (my[n, 0] + my[n, 1]) + (my[n, 2] + my[n, 3])
            for d in range(1, 4):
                push(mz.at[n, z], mz.at[n, z], m_send.at[1, n], m_recv.at[1, n], z_peer(d))

    own_copy.wait()

    def finish(p):
        @pl.when(p % 2 == 0)
        def _():
            n = p // 2
            wait_bytes(mz.at[n, pl.ds(0, 3)], m_recv.at[1, n])
            mass = (mz[n, 0] + mz[n, 1]) + (mz[n, 2] + mz[n, 3])
            mrep[1, 0:8, :] = mass

        mrep[0] = spread(mrep[1, pl.ds((p % 2) * 4 + z, 1), :])
        slack = EPS * arep[z, pl.ds(pl.multiple_of(p * CH + y * Q, Q), Q), :]
        a = 1.0 / (mrep[0, pl.ds(pl.multiple_of(y * Q, Q), Q), :] + slack)
        wait_bytes(u0.at[:, p], p_recv.at[8, p])
        wait_bytes(u1.at[:, p], p_recv.at[9, p])
        f0 = (s[0, z, p, y] + u0[0, p]) + (u0[1, p] + u0[2, p])
        f1 = (s[1, z, p, y] + u1[0, p]) + (u1[1, p] + u1[2, p])
        out_ref[p, :, 0:128] = (f0 + slack * cown[p, :, 0:128]) * a
        out_ref[p, :, 128:256] = (f1 + slack * cown[p, :, 128:256]) * a

    def final(n, carry):
        @pl.when(n < NP)
        def _():
            part(n)
            step_one(n)

        @pl.when((n >= LAG1) & (n < NP - DIRECT + LAG1))
        def _():
            step_two(n - LAG1)

        @pl.when((n >= LAG2) & (n < NP + LAG2))
        def _():
            step_three(n - LAG2)

        @pl.when(n >= LAG3)
        def _():
            finish(n - LAG3)

        return carry

    lax.fori_loop(0, NP + LAG3, final, 0)

    def drain_rows(r, carry):
        wait_bytes(rg0.at[r, pl.ds(0, 7)], r_send.at[0, r])
        wait_bytes(rg.at[0, r, pl.ds(0, 7)], r_send.at[1, r])
        wait_bytes(rg.at[1, r, pl.ds(0, 7)], r_send.at[2, r])
        wait_bytes(my.at[r, pl.ds(0, 3)], m_send.at[0, r])
        wait_bytes(mz.at[r, pl.ds(0, 3)], m_send.at[1, r])
        return carry

    lax.fori_loop(0, 4, drain_rows, 0)

    def drain_parts(p, carry):
        for n, ref in enumerate((ya, yb, za, zb, yc, yd, zc, zd)):
            wait_bytes(ref.at[p], p_send.at[n, p])
        wait_bytes(u0.at[:, p], p_send.at[8, p])
        wait_bytes(u1.at[:, p], p_send.at[9, p])
        return carry

    lax.fori_loop(0, NP, drain_parts, 0)
    for it in range(2):
        for b in range(4):
            wait_bytes(dg.at[it, b, pl.ds(0, 15)], d_send.at[it, b])


def local(vectors, codebook, cand_blocks, cand_counts):
    smem = pl.BlockSpec(memory_space=pltpu.SMEM)
    hbm = pl.BlockSpec(memory_space=pl.ANY)
    out = pl.pallas_call(
        kernel,
        out_shape=jax.ShapeDtypeStruct((NP, Q, 256), F32),
        in_specs=[smem, smem, hbm, hbm],
        out_specs=pl.BlockSpec(memory_space=pltpu.VMEM),
        scratch_shapes=[
            pltpu.VMEM((8, 1024, 1024), F32),
            pltpu.VMEM((2, 4, NP, 4, Q, 128), F32),
            pltpu.VMEM((4, 1024, 512), BF16),
            pltpu.VMEM((4, 1024, 256), BF16),
            pltpu.VMEM((4, 2048, 256), F8),
            pltpu.VMEM((4, 1024, 128), F32),
            pltpu.VMEM((4, 1024, 128), F32),
            pltpu.VMEM((8, 256, 256), F32),
            pltpu.VMEM((8, 256, 256), F32),
            pltpu.VMEM((NP, Q, 256), F32),
            pltpu.VMEM((4, 8, 1, 2048), F32),
            pltpu.VMEM((2, 4, 8, 1, 1024), F32),
            pltpu.VMEM((4, 1, 1024), F32),
            pltpu.VMEM((4, 1, 1024), F32),
            pltpu.VMEM((2, 4, 16, 8, 128), F32),
            pltpu.VMEM((4, 4, 8, 128), F32),
            pltpu.VMEM((4, 4, 8, 128), F32),
            pltpu.VMEM((2, 128, 128), F32),
            pltpu.VMEM((NP, 2, Q, 128), F32),
            pltpu.VMEM((NP, 2, Q, 128), F32),
            pltpu.VMEM((NP, 4, Q, 128), F32),
            pltpu.VMEM((NP, 4, Q, 128), F32),
            pltpu.VMEM((NP, 2, Q, 128), F32),
            pltpu.VMEM((NP, 2, Q, 128), F32),
            pltpu.VMEM((NP, 4, Q, 128), F32),
            pltpu.VMEM((NP, 4, Q, 128), F32),
            pltpu.VMEM((3, NP, Q, 128), F32),
            pltpu.VMEM((3, NP, Q, 128), F32),
            pltpu.SemaphoreType.DMA((3,)),
            pltpu.SemaphoreType.DMA((3, 4)),
            pltpu.SemaphoreType.DMA((3, 4)),
            pltpu.SemaphoreType.DMA((2, 4)),
            pltpu.SemaphoreType.DMA((2, 4)),
            pltpu.SemaphoreType.DMA((2, 4)),
            pltpu.SemaphoreType.DMA((2, 4)),
            pltpu.SemaphoreType.DMA((10, NP)),
            pltpu.SemaphoreType.DMA((10, NP)),
        ],
        compiler_params=pltpu.CompilerParams(
            collective_id=0, has_side_effects=True, vmem_limit_bytes=63 * 1024 * 1024,
        ),
    )(
        cand_blocks,
        cand_counts,
        vectors.reshape(4, 1024, 256),
        codebook.reshape(4, 4, NP, Q, 256),
    )
    return out.reshape(256, 256)


def solution(mesh):
    return jax.shard_map(
        local,
        mesh=mesh,
        in_specs=(P("dp", None), P("code", None), P("dp", "code", None), P("dp", "code")),
        out_specs=P(("code", "dp"), None),
        check_vma=False,
    )
```

time: 108 us -> 104 us (0.963)
  Pallas kernels: 104 us -> 99.1 us
    pallas_call x1, Pallas kernels: 104 us -> 99.1 us  [local(): pl.pallas_call(kernel, out_shape=jax.ShapeDtypeStruct((NP, Q, 256), F32),...]
where the time goes in v3:
time: 104 us; the launch traced here: 103 us
  Pallas kernels  99.1 us (95%)
  local copies, waits for them, and re-layouts  4.31 us (4%)
    pallas_call x1, Pallas kernels, local(): pl.pallas_call(kernel, out_shape=jax.ShapeDtypeStruct((NP, Q, 256), F32),...  99.1 us
    unnamed x3, local copies, waits for them, and re-layouts  4.31 us

profile of v3, /device:TPU:0, one launch (start us, length us, event | category | flops | bytes accessed | tf_op | source)
XLA Modules:
  0.0 103.4 jit_solution(8806808365562274730)
XLA Ops:
  0.0 1.3 %copy.5.blocks = s32[4,1,2]{2,1,0:T(1,128)} copy(s32[4,1,2]{0,2,1:T(2,128)} %param.6) | data formatting | bytes 64 | tf_op args[2]
  1.3 1.3 %copy.6.counts = s32[4,1]{1,0:T(4,128)} copy(s32[4,1]{0,1:T(1,128)} %param.7) | data formatting | bytes 32 | tf_op args[3]
  2.6 99.1 %shard_map.46 = f32[8,32,256]{2,1,0:T(8,128)} custom-call(s32[4,1,2]{2,1,0:T(1,128)} %copy.5.blocks, s32[4,1]{1,0:T(4,128)} %copy.6.counts, f32[4,1024,256]{2,1,0:T(8,128)} %bitcast.3, f32[4,4,8,32,256]{4,3,2,1,0:T(8,128)} %bitcast.4), custom_call_target="tpu_custom_call" | custom-call | tf_op jit(solution)/shard_map/pallas_call | solution.py:468
  101.8 1.7 %copy.8 = f32[256,256]{1,0:T(8,128)} copy(f32[256,256]{1,0:T(8,128)} %bitcast.5) | data formatting | bytes 524288

commit v4 on v3

--- a/solution.py
+++ b/solution.py
@@ -53,7 +53,9 @@
     raws = (raw0, raw1)
 
     code_peers = [(dp, (code + d) % 8) for d in range(8)]
-    dp_peers = [((dp + d) % 16, code) for d in range(16)]
+    steps = [(a, b) for a in range(4) for b in range(4) if a or b]
+    steps.sort(key=lambda s: -(min(s[0], 4 - s[0]) + min(s[1], 4 - s[1])))
+    dp_peers = [(((z + a) % 4) * 4 + (y + b) % 4, code) for a, b in steps]
 
     def z_peer(d):
         return (((z + d) % 4) * 4 + y, code)
@@ -78,27 +80,28 @@
     own_copy.start()
 
     barrier = pltpu.get_barrier_semaphore()
-    for d in range(1, 8):
+    for d in (4, 3, 5, 2, 6, 1, 7):
         pl.semaphore_signal(barrier, inc=1, device_id=code_peers[d], device_id_type=MESH)
-    for d in range(1, 16):
+    for d in range(15):
         pl.semaphore_signal(barrier, inc=1, device_id=dp_peers[d], device_id_type=MESH)
 
     wait_bytes(s, c_sem.at[0])
 
     def prepare(n, carry):
-        b, p = n // NP, n % NP
-        c0 = s[0, b, p].reshape(CH, 128)
-        c1 = s[1, b, p].reshape(CH, 128)
+        b, p = n // 2, n % 2
+        half = pl.ds(p * (NP // 2), NP // 2)
+        c0 = s[0, b, half].reshape(512, 128)
+        c1 = s[1, b, half].reshape(512, 128)
         norm = jnp.sum(c0 * c0 + c1 * c1, axis=1, keepdims=True) * (-0.25 * LOG2E)
-        rows = pl.ds(pl.multiple_of(p * CH, CH), CH)
-        bias[b, rows, :] = jnp.broadcast_to(norm, (CH, 128))
+        rows = pl.ds(pl.multiple_of(p * 512, 512), 512)
+        bias[b, rows, :] = jnp.broadcast_to(norm, (512, 128))
         for h, part in enumerate((c0, c1)):
             hi, lo = split(part * (0.5 * LOG2E))
             ccat[b, rows, h * 128:(h + 1) * 128] = hi
             ccat[b, rows, 256 + h * 128:256 + (h + 1) * 128] = lo
         return carry
 
-    lax.fori_loop(0, 4 * NP, prepare, 0)
+    lax.fori_loop(0, 8, prepare, 0)
     wait_bytes(e.at[7], c_sem.at[1])
 
     def score(r, iq):
@@ -143,7 +146,7 @@
         rg0[r, code, :, 1024 + iq * 256:1280 + iq * 256] = jnp.sum(total, axis=0, keepdims=True)
 
     def send_first(r):
-        for d in range(1, 8):
+        for d in (4, 3, 5, 2, 6, 1, 7):
             push(rg0.at[r, code], rg0.at[r, code], r_send.at[0, r], r_recv.at[0, r], code_peers[d])
 
     score(0, 0)
@@ -221,7 +224,7 @@
 
                 acc = lax.fori_loop(0, 4, chunk, acc)
             rg[it, r, code] = jnp.sum(acc, axis=0, keepdims=True) * alpha[r]
-            for d in range(1, 8):
+            for d in (4, 3, 5, 2, 6, 1, 7):
                 push(
                     rg.at[it, r, code], rg.at[it, r, code],
                     r_send.at[it + 1, r], r_recv.at[it + 1, r], code_peers[d],
@@ -245,7 +248,7 @@
                     total = total + jnp.where(has, s[r // 2, (r % 2) * 2 + slot, p], 0.0)
                 row = jnp.sum(total.reshape(128, 128).T, axis=0, keepdims=True)
                 dg[it, b, dp, p:p + 1, :] = row
-            for d in range(1, 16):
+            for d in range(15):
                 push(dg.at[it, b, dp], dg.at[it, b, dp], d_send.at[it, b], d_recv.at[it, b], dp_peers[d])
             return carry
 
@@ -300,7 +303,7 @@
                 raw0[r * 2 + slot, 0:CH, :] = value[slot * CH:(slot + 1) * CH]
             return carry
 
-        lax.fori_loop(0, 4, one, 0)
+        lax.fori_loop(0, 4, one, 0, unroll=2)
         for b in range(4):
             total = jnp.zeros((CH, 256), F32)
             mass = jnp.zeros((CH, 128), F32)

time: 104 us -> 99.6 us (0.958)
  Pallas kernels: 99.1 us -> 95.1 us
    pallas_call x1, Pallas kernels: 99.1 us -> 95.1 us  [local(): pl.pallas_call(kernel, out_shape=jax.ShapeDtypeStruct((NP, Q, 256), F32),...]
where the time goes in v4:
time: 99.6 us; the launch traced here: 99.4 us
  Pallas kernels  95.1 us (95%)
  local copies, waits for them, and re-layouts  4.31 us (4%)
    pallas_call x1, Pallas kernels, local(): pl.pallas_call(kernel, out_shape=jax.ShapeDtypeStruct((NP, Q, 256), F32),...  95.1 us
    unnamed x3, local copies, waits for them, and re-layouts  4.31 us

profile of v4, /device:TPU:0, one launch (start us, length us, event | category | flops | bytes accessed | tf_op | source)
XLA Modules:
  0.0 99.4 jit_solution(7719992070787842830)
XLA Ops:
  0.0 1.3 %copy.5.blocks = s32[4,1,2]{2,1,0:T(1,128)} copy(s32[4,1,2]{0,2,1:T(2,128)} %param.6) | data formatting | bytes 64 | tf_op args[2]
  1.3 1.3 %copy.6.counts = s32[4,1]{1,0:T(4,128)} copy(s32[4,1]{0,1:T(1,128)} %param.7) | data formatting | bytes 32 | tf_op args[3]
  2.6 95.1 %shard_map.46 = f32[8,32,256]{2,1,0:T(8,128)} custom-call(s32[4,1,2]{2,1,0:T(1,128)} %copy.5.blocks, s32[4,1]{1,0:T(4,128)} %copy.6.counts, f32[4,1024,256]{2,1,0:T(8,128)} %bitcast.3, f32[4,4,8,32,256]{4,3,2,1,0:T(8,128)} %bitcast.4), custom_call_target="tpu_custom_call" | custom-call | tf_op jit(solution)/shard_map/pallas_call | solution.py:471
  97.8 1.7 %copy.8 = f32[256,256]{1,0:T(8,128)} copy(f32[256,256]{1,0:T(8,128)} %bitcast.5) | data formatting | bytes 524288

commit v5 on v4

--- a/solution.py
+++ b/solution.py
@@ -303,7 +303,7 @@
                 raw0[r * 2 + slot, 0:CH, :] = value[slot * CH:(slot + 1) * CH]
             return carry
 
-        lax.fori_loop(0, 4, one, 0, unroll=2)
+        lax.fori_loop(0, 4, one, 0, unroll=4)
         for b in range(4):
             total = jnp.zeros((CH, 256), F32)
             mass = jnp.zeros((CH, 128), F32)

time: 99.6 us -> 99.1 us (level)
  no operation moved by 1% of the time
where the time goes in v5:
time: 99.1 us; the launch traced here: 98.9 us
  Pallas kernels  94.6 us (95%)
  local copies, waits for them, and re-layouts  4.31 us (4%)
    pallas_call x1, Pallas kernels, local(): pl.pallas_call(kernel, out_shape=jax.ShapeDtypeStruct((NP, Q, 256), F32),...  94.6 us
    unnamed x3, local copies, waits for them, and re-layouts  4.31 us

profile of v5, /device:TPU:0, one launch (start us, length us, event | category | flops | bytes accessed | tf_op | source)
XLA Modules:
  0.0 98.9 jit_solution(16660594308328510828)
XLA Ops:
  0.0 1.3 %copy.5.blocks = s32[4,1,2]{2,1,0:T(1,128)} copy(s32[4,1,2]{0,2,1:T(2,128)} %param.6) | data formatting | bytes 64 | tf_op args[2]
  1.3 1.3 %copy.6.counts = s32[4,1]{1,0:T(4,128)} copy(s32[4,1]{0,1:T(1,128)} %param.7) | data formatting | bytes 32 | tf_op args[3]
  2.6 94.6 %shard_map.46 = f32[8,32,256]{2,1,0:T(8,128)} custom-call(s32[4,1,2]{2,1,0:T(1,128)} %copy.5.blocks, s32[4,1]{1,0:T(4,128)} %copy.6.counts, f32[4,1024,256]{2,1,0:T(8,128)} %bitcast.3, f32[4,4,8,32,256]{4,3,2,1,0:T(8,128)} %bitcast.4), custom_call_target="tpu_custom_call" | custom-call | tf_op jit(solution)/shard_map/pallas_call | solution.py:471
  97.2 1.7 %copy.8 = f32[256,256]{1,0:T(8,128)} copy(f32[256,256]{1,0:T(8,128)} %bitcast.5) | data formatting | bytes 524288
